TPU v7x, 256 devices: a whole 4x4x8 slice. The times are simulated.
256 devices in a mesh: row: 32 (over y, z), col: 8 (over x, core).
Axes of the slice: x: 4, y: 4, z: 8, core: 2. Of those that a mesh axis runs over, the one named last changes fastest.
Arguments:
- krylov: bfloat16 [2048, 512], P(('row', 'col')), may hold values from -6 to 6
- jacobian_tiles: bfloat16 [49152, 128, 128], P(('row', 'col')), may hold values from -0.5 to 0.5
- tile_rows: int32 [49152], P(('row', 'col')), may hold values from 0 to 63
- tile_cols: int32 [49152], P(('row', 'col')), may hold values from 0 to 255
- live_tiles: int32 [256], P(('row', 'col')), may hold values from 1 to 192, as said below
Outputs:
- adjoint_image: float32 [2048, 512], P(('col', 'row'))
Inputs may be any that keep to these rules, and one draw needn't show every extreme that they name: `live_tiles`: each device has at least one used slot; in every draw some device uses all 192 slots.
All inputs are finite; a program needn't handle non-finite values.
Results may differ from a plain program's by a relative error of at most 0.0003.
Values may be sent and summed in bfloat16 or wider, within the bound.
No kernel may reach another device: no remote copies, remote signals or barrier semaphores. Data moves between devices by JAX's collectives and lax.ppermute only.
A program may use at most 64 MiB of HBM per device.

v0:
```python
import functools

import jax
import jax.numpy as jnp
from jax import lax
from jax.experimental import pallas as pl
from jax.experimental.pallas import tpu as pltpu
from jax.sharding import PartitionSpec as P

TILE = 128
SUB = 8
GROUP = 48
HOPS = (1, 2, 3)
F32 = jnp.float32


def join_kernel(*refs):
    *part_refs, tiles_ref, out_ref = refs
    for i, part_ref in enumerate(part_refs):
        out_ref[i] = part_ref[...]


def contribution_kernel(live_ref, *refs):
    index_refs, refs = refs[:2], refs[2:]
    pair_ref, joined_ref, tiles_ref, out_ref, x_ref, sum_ref, rows_ref, cols_ref, sems = refs
    copies = [
        pltpu.make_async_copy(source, target, sems.at[i])
        for i, (source, target) in enumerate(zip(index_refs, (rows_ref, cols_ref)))
    ]
    for copy in copies:
        copy.start()
    rows, row_width = pair_ref.shape[0] // 2, pair_ref.shape[1]
    vectors = row_width // TILE
    chips = joined_ref.shape[0] + 1
    words = vectors // 2 * SUB
    pairs = tiles_ref.shape[0]
    blocks = 2 * chips * rows
    me = lax.axis_index("col")
    live = live_ref[0]
    x_ref[...] = jnp.zeros_like(x_ref)
    sum_ref[...] = jnp.zeros_like(sum_ref)
    for hop in range(chips):
        chip = (me // 2) ^ hop
        for part in range(2):
            holder = 2 * chip + lax.rem(me + part, 2)
            base = pl.multiple_of(holder * rows * SUB, rows * SUB)
            for v in range(vectors):
                window = (pl.ds(part * rows, rows), pl.ds(v * TILE, TILE))
                column = pair_ref[window] if hop == 0 else joined_ref[(hop - 1, *window)]
                column = column.astype(F32)
                x_ref[0, pl.ds(base + v, rows, stride=SUB), :] = column
                x_ref[1, pl.ds(base + vectors + v, rows, stride=SUB), :] = column

    for copy in copies:
        copy.wait()

    for step in range(pairs // GROUP):
        products = []
        for k in range(GROUP):
            pair = step * GROUP + k
            halves = []
            for half in range(2):
                slot = 2 * pair + half
                row = jnp.where(slot < live, rows_ref[slot], blocks)
                start = pl.multiple_of(row * SUB, SUB)
                halves.append(x_ref[half, pl.ds(start, SUB), :])
            left = jnp.concatenate(halves, axis=1).astype(jnp.bfloat16)
            products.append(jnp.dot(left, tiles_ref[pair], preferred_element_type=F32))
        for k in range(GROUP):
            pair = step * GROUP + k
            for half in range(2):
                start = pl.multiple_of(cols_ref[2 * pair + half] * SUB, SUB)
                place = pl.ds(start + half * vectors, vectors)
                sum_ref[place, :] += products[k][half * vectors : (half + 1) * vectors, :]

    peers = out_ref.shape[0] // (words + 1)
    own = sum_ref.shape[0] // peers
    for peer in range(peers):
        base, first_row = peer * own, peer * (words + 1)
        totals = []
        for v in range(vectors):
            first = sum_ref[pl.ds(base + v, SUB, stride=SUB), :]
            second = sum_ref[pl.ds(base + vectors + v, SUB, stride=SUB), :]
            totals.append(first + second)
        peaks = functools.reduce(jnp.maximum, [jnp.abs(total) for total in totals])
        peak = jnp.max(peaks, axis=0, keepdims=True)
        power = jnp.ceil(jnp.log2(jnp.maximum(peak, 2.0**-111)) + 0.01)
        scale = jnp.exp2(15.0 - power)
        codes = [jnp.round(total * scale).astype(jnp.int32) for total in totals]
        for half in range(vectors // 2):
            word = (codes[2 * half] << 16) | (codes[2 * half + 1] & 0xFFFF)
            out_ref[first_row + half * SUB : first_row + (half + 1) * SUB, :] = word
        out_ref[first_row + words : first_row + words + 1, :] = power.astype(jnp.int32)


def sum_kernel(in_ref, out_ref):
    vectors = out_ref.shape[1] // TILE
    words = vectors // 2 * SUB
    peers = in_ref.shape[0] // (words + 1)
    totals = [jnp.zeros((SUB, TILE), F32) for _ in range(vectors)]
    for peer in range(peers):
        first_row = peer * (words + 1)
        row = in_ref[first_row + words : first_row + words + 1, :]
        scale = jnp.exp2(row.astype(F32) - 15.0)
        for half in range(vectors // 2):
            word = in_ref[first_row + half * SUB : first_row + (half + 1) * SUB, :]
            totals[2 * half] += (word >> 16).astype(F32) * scale
            totals[2 * half + 1] += ((word << 16) >> 16).astype(F32) * scale
    out_ref[...] = jnp.concatenate(totals, axis=1)


def per_device(krylov, jacobian_tiles, tile_rows, tile_cols, live_tiles):
    col_count = lax.axis_size("col")
    row_count = lax.axis_size("row")
    chips = col_count // 2
    own_rows, row_width = krylov.shape
    slots = jacobian_tiles.shape[0]
    vectors = row_width // TILE
    words = vectors // 2 * SUB
    smem = pl.BlockSpec(memory_space=pltpu.SMEM)
    vmem = pl.BlockSpec(memory_space=pltpu.VMEM)

    other = lax.ppermute(krylov, "col", [(i, i ^ 1) for i in range(col_count)])
    pair = jnp.concatenate([krylov, other])
    far = [None] * chips
    for hop in HOPS:
        steps = [(i, i ^ (2 * hop)) for i in range(col_count)]
        far[hop] = lax.ppermute(pair, "col", steps)
    tiles = jacobian_tiles.reshape(slots // 2, 2 * TILE, TILE)
    joined = pl.pallas_call(
        join_kernel,
        out_shape=jax.ShapeDtypeStruct((chips - 1, 2 * own_rows, row_width), krylov.dtype),
        in_specs=[vmem] * (chips - 1) + [pl.BlockSpec(memory_space=pltpu.HBM)],
        out_specs=vmem,
        compiler_params=pltpu.CompilerParams(vmem_limit_bytes=2**20),
        cost_estimate=pl.CostEstimate(flops=0, bytes_accessed=4 * jacobian_tiles.size, transcendentals=0),
    )(*far[1:], pltpu.with_memory_space_constraint(tiles, pltpu.HBM))
    coded = pl.pallas_call(
        contribution_kernel,
        out_shape=jax.ShapeDtypeStruct((row_count * (words + 1), TILE), jnp.int32),
        in_specs=[smem] + [vmem] * 5,
        out_specs=vmem,
        scratch_shapes=[
            pltpu.VMEM((2, (own_rows * col_count + 1) * SUB, TILE), F32),
            pltpu.VMEM((row_count * own_rows * SUB, TILE), F32),
            pltpu.SMEM(tile_rows.shape, tile_rows.dtype),
            pltpu.SMEM(tile_cols.shape, tile_cols.dtype),
            pltpu.SemaphoreType.DMA((2,)),
        ],
        compiler_params=pltpu.CompilerParams(vmem_limit_bytes=10 * 2**20),
    )(live_tiles, tile_rows, tile_cols, pair, joined, tiles)
    pieces = coded.reshape(row_count, words + 1, 1, TILE)
    received = lax.all_to_all(pieces, "row", 0, 0).reshape(coded.shape)
    return pl.pallas_call(
        sum_kernel,
        out_shape=jax.ShapeDtypeStruct((own_rows, row_width), F32),
        in_specs=[vmem],
        out_specs=vmem,
        compiler_params=pltpu.CompilerParams(vmem_limit_bytes=4 * 2**20),
    )(received)


def solution(mesh):
    placed = (
        P(("row", "col"), None),
        P(("row", "col"), None, None),
        P(("row", "col")),
        P(("row", "col")),
        P(("row", "col")),
    )
    return jax.shard_map(
        per_device, mesh=mesh, in_specs=placed, out_specs=P(("col", "row"), None), check_vma=False
    )
```

profile of v0, /device:TPU:32, one launch (start us, length us, event | category | flops | bytes accessed | tf_op | source)
XLA Modules:
  0.0 34.8 jit_solution(17918236915906986652)
XLA Ops:
  0.0 0.0 copy-start
  0.0 0.0 copy-start.2
  0.0 0.0 copy-start.1
  0.0 0.1 collective-permute-start
  0.1 0.8 %constant_dynamic-update-slice_fusion.1 = bf16[16,512]{1,0:T(8,128)(2,1)S(1)} fusion(bf16[8,512]{1,0:T(8,128)(2,1)} %param.5), kind=kLoop, calls=%fused_computation.1 | loop fusion | bytes 16384
  1.0 0.5 %collective-permute-done = bf16[8,512]{1,0:T(8,128)(2,1)S(1)} collective-permute-done((bf16[8,512]{1,0:T(8,128)(2,1)}, bf16[8,512]{1,0:T(8,128)(2,1)S(1)}, u32[]{:S(2)}, u32[]{:S(2)}) %collective-permute-start) | collective-permute-done | bytes 8224 | tf_op jit(solution)/shard_map/ppermute | solution.py:123
  1.5 2.8 %collective-permute-start.3 = (bf16[16,512]{1,0:T(8,128)(2,1)S(1)}, bf16[16,512]{1,0:T(8,128)(2,1)S(1)}, u32[]{:S(2)}, u32[]{:S(2)}) collective-permute-start(bf16[16,512]{1,0:T(8,128)(2,1)S(1)} %constant_dynamic-update-slice_fusion.refs_2_), channel_id=1, source_target_pairs={{0,6},{1,7},{2,4},{3,5},{4,2},{5,3},{6,0},{7,1},{8,14},{9,15},{10,... | collective-permute-start | bytes 49160 | tf_op jit(solution)/shard_map/ppermute | solution.py:128
  4.2 0.8 %collective-permute-start.2 = (bf16[16,512]{1,0:T(8,128)(2,1)S(1)}, bf16[16,512]{1,0:T(8,128)(2,1)S(1)}, u32[]{:S(2)}, u32[]{:S(2)}) collective-permute-start(bf16[16,512]{1,0:T(8,128)(2,1)S(1)} %constant_dynamic-update-slice_fusion.refs_2_), channel_id=1, source_target_pairs={{0,4},{1,5},{2,6},{3,7},{4,0},{5,1},{6,2},{7,3},{8,12},{9,13},{10,... | collective-permute-start | bytes 49160 | tf_op jit(solution)/shard_map/ppermute | solution.py:128
  5.0 0.5 %collective-permute-start.1 = (bf16[16,512]{1,0:T(8,128)(2,1)S(1)}, bf16[16,512]{1,0:T(8,128)(2,1)S(1)}, u32[]{:S(2)}, u32[]{:S(2)}) collective-permute-start(bf16[16,512]{1,0:T(8,128)(2,1)S(1)} %constant_dynamic-update-slice_fusion.refs_2_), channel_id=1, source_target_pairs={{0,2},{1,3},{2,0},{3,1},{4,6},{5,7},{6,4},{7,5},{8,10},{9,11},{10,... | collective-permute-start | bytes 49160 | tf_op jit(solution)/shard_map/ppermute | solution.py:128
  6.2 0.2 collective-permute-done.3.refs_2_
  6.4 3.1 %collective-permute-done.2.refs_1_ = bf16[16,512]{1,0:T(8,128)(2,1)S(1)} collective-permute-done((bf16[16,512]{1,0:T(8,128)(2,1)S(1)}, bf16[16,512]{1,0:T(8,128)(2,1)S(1)}, u32[]{:S(2)}, u32[]{:S(2)}) %collective-permute-start.2) | collective-permute-done | bytes 16416 | tf_op jit(solution)/shard_map/ppermute | solution.py:128
  9.5 0.0 collective-permute-done.1.refs_0_
  9.5 0.0 copy-done
  9.5 0.0 copy-done.2
  9.5 0.0 copy-done.1
  9.5 1.9 %shard_map.56 = s32[544,128]{1,0:T(8,128)S(1)} custom-call(s32[1]{0:T(128)S(6)} %copy.8.live_ref, s32[192]{0:T(256)S(1)} %copy-done.1, s32[192]{0:T(256)S(1)} %copy-done.2, bf16[16,512]{1,0:T(8,128)(2,1)S(1)} %constant_dynamic-update-slice_fusion.refs_2_, bf16[3,16,512]{2,1,0:T(8,128)(2,1)S(1)} %shard_map.55.refs_3_, bf16[96,256,128]{2,1,0:T(8,128)(2,1)S(1)} %bitcast.4), custom_call_target="tpu_custom_call" | custom-call | tf_op jit(solution)/shard_map/pallas_call | solution.py:138
  11.4 22.7 %all_to_all.5 = s32[32,17,1,128]{3,2,1,0:T(1,128)S(1)} all-to-all(s32[32,17,1,128]{3,2,1,0:T(1,128)S(1)} %bitcast.5), channel_id=1, replica_groups=mesh['row'=32,'col'=8] {'row'}, dimensions={0} | all-to-all | bytes 557056 | tf_op jit(solution)/shard_map/all_to_all | solution.py:153
  34.1 0.7 %shard_map.57 = f32[8,512]{1,0:T(8,128)} custom-call(s32[544,128]{1,0:T(8,128)S(1)} %bitcast.6), custom_call_target="tpu_custom_call" | custom-call | tf_op jit(solution)/shard_map/pallas_call | solution.py:154
  (2 shorter events, 0.0 us)
Async XLA Ops:
  0.0 9.5 %copy-start = (bf16[192,128,128]{2,1,0:T(8,128)(2,1)S(1)}, bf16[192,128,128]{2,1,0:T(8,128)(2,1)}, u32[]{:S(2)}) copy-start(bf16[192,128,128]{2,1,0:T(8,128)(2,1)} %param.6) | copy-start | bytes 18874372
  0.0 9.5 %copy-start.2 = (s32[192]{0:T(256)S(1)}, s32[192]{0:T(256)}, u32[]{:S(2)}) copy-start(s32[192]{0:T(256)} %refs_1_.1) | copy-start | bytes 2308
  0.0 9.5 %copy-start.1 = (s32[192]{0:T(256)S(1)}, s32[192]{0:T(256)}, u32[]{:S(2)}) copy-start(s32[192]{0:T(256)} %refs_0_.1) | copy-start | bytes 2308
  0.0 1.5 %collective-permute-start = (bf16[8,512]{1,0:T(8,128)(2,1)}, bf16[8,512]{1,0:T(8,128)(2,1)S(1)}, u32[]{:S(2)}, u32[]{:S(2)}) collective-permute-start(bf16[8,512]{1,0:T(8,128)(2,1)} %param.5), channel_id=1, source_target_pairs={{0,1},{1,0},{2,3},{3,2},{4,5},{5,4},{6,7},{7,6},{8,9},{9,8},{10,11... | collective-permute-start | bytes 24584 | tf_op jit(solution)/shard_map/ppermute | solution.py:123
  1.5 4.9 %collective-permute-start.3 = (bf16[16,512]{1,0:T(8,128)(2,1)S(1)}, bf16[16,512]{1,0:T(8,128)(2,1)S(1)}, u32[]{:S(2)}, u32[]{:S(2)}) collective-permute-start(bf16[16,512]{1,0:T(8,128)(2,1)S(1)} %constant_dynamic-update-slice_fusion.refs_2_), channel_id=1, source_target_pairs={{0,6},{1,7},{2,4},{3,5},{4,2},{5,3},{6,0},{7,1},{8,14},{9,15},{10,... | collective-permute-start | bytes 49160 | tf_op jit(solution)/shard_map/ppermute | solution.py:128
  4.2 5.2 %collective-permute-start.2 = (bf16[16,512]{1,0:T(8,128)(2,1)S(1)}, bf16[16,512]{1,0:T(8,128)(2,1)S(1)}, u32[]{:S(2)}, u32[]{:S(2)}) collective-permute-start(bf16[16,512]{1,0:T(8,128)(2,1)S(1)} %constant_dynamic-update-slice_fusion.refs_2_), channel_id=1, source_target_pairs={{0,4},{1,5},{2,6},{3,7},{4,0},{5,1},{6,2},{7,3},{8,12},{9,13},{10,... | collective-permute-start | bytes 49160 | tf_op jit(solution)/shard_map/ppermute | solution.py:128
  5.0 4.4 %collective-permute-start.1 = (bf16[16,512]{1,0:T(8,128)(2,1)S(1)}, bf16[16,512]{1,0:T(8,128)(2,1)S(1)}, u32[]{:S(2)}, u32[]{:S(2)}) collective-permute-start(bf16[16,512]{1,0:T(8,128)(2,1)S(1)} %constant_dynamic-update-slice_fusion.refs_2_), channel_id=1, source_target_pairs={{0,2},{1,3},{2,0},{3,1},{4,6},{5,7},{6,4},{7,5},{8,10},{9,11},{10,... | collective-permute-start | bytes 49160 | tf_op jit(solution)/shard_map/ppermute | solution.py:128
where the time goes:
time: 35 us; the launch traced here: 34.8 us
  blocking collectives  22.7 us (65%)
  starting transfers between devices  4.19 us (12%)
  waiting for transfers between devices  3.78 us (11%)
  Pallas kernels  2.63 us (8%)
  local copies, waits for them, and re-layouts  0.86 us (2%)
  between operations  0.7 us (2%)
    all_to_all x1, blocking collectives, per_device(): received = lax.all_to_all(pieces, 'row', 0, 0).reshape(coded.shape)  22.7 us
    ppermute x3, starting transfers between devices, per_device(): far[hop] = lax.ppermute(pair, 'col', steps)  4.09 us
    ppermute x3, waiting for transfers between devices, per_device(): far[hop] = lax.ppermute(pair, 'col', steps)  3.26 us
    pallas_call x1, Pallas kernels, per_device(): pl.pallas_call(contribution_kernel, out_shape=jax.ShapeDtypeStruct((row_c...  1.92 us
    unnamed x7, local copies, waits for them, and re-layouts  0.86 us
    pallas_call x1, Pallas kernels, per_device(): pl.pallas_call(sum_kernel, out_shape=jax.ShapeDtypeStruct((own_rows, row_...  0.71 us
  transfers between devices with their start and end apart: 4, of which 3 were waited for; matrix products, arithmetic and copies ran while one was open for 2% of the time, Pallas kernels for 0%

commit v1 on v0

--- a/solution.py
+++ b/solution.py
@@ -10,6 +10,7 @@
 TILE = 128
 SUB = 8
 GROUP = 48
+PEERS = [4, 12, 24, 2, 28, 10, 18, 27, 21, 9, 19, 8, 6, 17, 13, 15, 29, 3, 5, 1, 7, 14, 0, 31, 20, 30, 26, 22, 25, 11, 23, 16]
 HOPS = (1, 2, 3)
 F32 = jnp.float32
 
@@ -76,7 +77,7 @@
     peers = out_ref.shape[0] // (words + 1)
     own = sum_ref.shape[0] // peers
     for peer in range(peers):
-        base, first_row = peer * own, peer * (words + 1)
+        base, first_row = PEERS[peer] * own, peer * (words + 1)
         totals = []
         for v in range(vectors):
             first = sum_ref[pl.ds(base + v, SUB, stride=SUB), :]
@@ -150,7 +151,7 @@
         compiler_params=pltpu.CompilerParams(vmem_limit_bytes=10 * 2**20),
     )(live_tiles, tile_rows, tile_cols, pair, joined, tiles)
     pieces = coded.reshape(row_count, words + 1, 1, TILE)
-    received = lax.all_to_all(pieces, "row", 0, 0).reshape(coded.shape)
+    received = lax.all_to_all(pieces, "row", 0, 0, axis_index_groups=[PEERS]).reshape(coded.shape)
     return pl.pallas_call(
         sum_kernel,
         out_shape=jax.ShapeDtypeStruct((own_rows, row_width), F32),

time: 35 us -> 32.9 us (0.940)
  blocking collectives: 22.7 us -> 20.6 us
    all_to_all x1, blocking collectives: 22.7 us -> 20.6 us  [per_device(): lax.all_to_all(pieces, 'row', 0, 0, axis_index_groups=[PEERS])]
  transfers between devices with their start and end apart: 4 -> 4, of which waited for: 3 -> 3; matrix products, arithmetic and copies ran while one was open for 2% -> 3% of each run, Pallas kernels for 0% -> 0%
where the time goes in v1:
time: 32.9 us; the launch traced here: 32.7 us
  blocking collectives  20.6 us (63%)
  starting transfers between devices  4.19 us (13%)
  waiting for transfers between devices  3.78 us (11%)
  Pallas kernels  2.63 us (8%)
  local copies, waits for them, and re-layouts  0.86 us (3%)
  between operations  0.7 us (2%)
    all_to_all x1, blocking collectives, per_device(): lax.all_to_all(pieces, 'row', 0, 0, axis_index_groups=[PEERS])  20.6 us
    ppermute x3, starting transfers between devices, per_device(): far[hop] = lax.ppermute(pair, 'col', steps)  4.09 us
    ppermute x3, waiting for transfers between devices, per_device(): far[hop] = lax.ppermute(pair, 'col', steps)  3.26 us
    pallas_call x1, Pallas kernels, per_device(): pl.pallas_call(contribution_kernel, out_shape=jax.ShapeDtypeStruct((row_c...  1.92 us
    unnamed x7, local copies, waits for them, and re-layouts  0.86 us
    pallas_call x1, Pallas kernels, per_device(): pl.pallas_call(sum_kernel, out_shape=jax.ShapeDtypeStruct((own_rows, row_...  0.71 us
  transfers between devices with their start and end apart: 4, of which 3 were waited for; matrix products, arithmetic and copies ran while one was open for 3% of the time, Pallas kernels for 0%

profile of v1, /device:TPU:32, one launch (start us, length us, event | category | flops | bytes accessed | tf_op | source)
XLA Modules:
  0.0 32.7 jit_solution(4816435043947022901)
XLA Ops:
  0.0 0.0 copy-start
  0.0 0.0 copy-start.2
  0.0 0.0 copy-start.1
  0.0 0.1 collective-permute-start
  0.1 0.8 %constant_dynamic-update-slice_fusion.1 = bf16[16,512]{1,0:T(8,128)(2,1)S(1)} fusion(bf16[8,512]{1,0:T(8,128)(2,1)} %param.5), kind=kLoop, calls=%fused_computation.1 | loop fusion | bytes 16384
  1.0 0.5 %collective-permute-done = bf16[8,512]{1,0:T(8,128)(2,1)S(1)} collective-permute-done((bf16[8,512]{1,0:T(8,128)(2,1)}, bf16[8,512]{1,0:T(8,128)(2,1)S(1)}, u32[]{:S(2)}, u32[]{:S(2)}) %collective-permute-start) | collective-permute-done | bytes 8224 | tf_op jit(solution)/shard_map/ppermute | solution.py:124
  1.5 2.8 %collective-permute-start.3 = (bf16[16,512]{1,0:T(8,128)(2,1)S(1)}, bf16[16,512]{1,0:T(8,128)(2,1)S(1)}, u32[]{:S(2)}, u32[]{:S(2)}) collective-permute-start(bf16[16,512]{1,0:T(8,128)(2,1)S(1)} %constant_dynamic-update-slice_fusion.refs_2_), channel_id=1, source_target_pairs={{0,6},{1,7},{2,4},{3,5},{4,2},{5,3},{6,0},{7,1},{8,14},{9,15},{10,... | collective-permute-start | bytes 49160 | tf_op jit(solution)/shard_map/ppermute | solution.py:129
  4.2 0.8 %collective-permute-start.2 = (bf16[16,512]{1,0:T(8,128)(2,1)S(1)}, bf16[16,512]{1,0:T(8,128)(2,1)S(1)}, u32[]{:S(2)}, u32[]{:S(2)}) collective-permute-start(bf16[16,512]{1,0:T(8,128)(2,1)S(1)} %constant_dynamic-update-slice_fusion.refs_2_), channel_id=1, source_target_pairs={{0,4},{1,5},{2,6},{3,7},{4,0},{5,1},{6,2},{7,3},{8,12},{9,13},{10,... | collective-permute-start | bytes 49160 | tf_op jit(solution)/shard_map/ppermute | solution.py:129
  5.0 0.5 %collective-permute-start.1 = (bf16[16,512]{1,0:T(8,128)(2,1)S(1)}, bf16[16,512]{1,0:T(8,128)(2,1)S(1)}, u32[]{:S(2)}, u32[]{:S(2)}) collective-permute-start(bf16[16,512]{1,0:T(8,128)(2,1)S(1)} %constant_dynamic-update-slice_fusion.refs_2_), channel_id=1, source_target_pairs={{0,2},{1,3},{2,0},{3,1},{4,6},{5,7},{6,4},{7,5},{8,10},{9,11},{10,... | collective-permute-start | bytes 49160 | tf_op jit(solution)/shard_map/ppermute | solution.py:129
  6.2 0.2 collective-permute-done.3.refs_2_
  6.4 3.1 %collective-permute-done.2.refs_1_ = bf16[16,512]{1,0:T(8,128)(2,1)S(1)} collective-permute-done((bf16[16,512]{1,0:T(8,128)(2,1)S(1)}, bf16[16,512]{1,0:T(8,128)(2,1)S(1)}, u32[]{:S(2)}, u32[]{:S(2)}) %collective-permute-start.2) | collective-permute-done | bytes 16416 | tf_op jit(solution)/shard_map/ppermute | solution.py:129
  9.5 0.0 collective-permute-done.1.refs_0_
  9.5 0.0 copy-done
  9.5 0.0 copy-done.2
  9.5 0.0 copy-done.1
  9.5 1.9 %shard_map.56 = s32[544,128]{1,0:T(8,128)S(1)} custom-call(s32[1]{0:T(128)S(6)} %copy.8.live_ref, s32[192]{0:T(256)S(1)} %copy-done.1, s32[192]{0:T(256)S(1)} %copy-done.2, bf16[16,512]{1,0:T(8,128)(2,1)S(1)} %constant_dynamic-update-slice_fusion.refs_2_, bf16[3,16,512]{2,1,0:T(8,128)(2,1)S(1)} %shard_map.55.refs_3_, bf16[96,256,128]{2,1,0:T(8,128)(2,1)S(1)} %bitcast.4), custom_call_target="tpu_custom_call" | custom-call | tf_op jit(solution)/shard_map/pallas_call | solution.py:139
  11.5 20.6 %all_to_all.5 = s32[32,17,1,128]{3,2,1,0:T(1,128)S(1)} all-to-all(s32[32,17,1,128]{3,2,1,0:T(1,128)S(1)} %bitcast.5), channel_id=1, replica_groups={{32,96,192,16,224,80,144,216,168,72,152,64,48,136,104,120,232,24,40,8,5..., dimensions={0} | all-to-all | bytes 557056 | tf_op jit(solution)/shard_map/all_to_all | solution.py:154
  32.0 0.7 %shard_map.57 = f32[8,512]{1,0:T(8,128)} custom-call(s32[544,128]{1,0:T(8,128)S(1)} %bitcast.6), custom_call_target="tpu_custom_call" | custom-call | tf_op jit(solution)/shard_map/pallas_call | solution.py:155
  (2 shorter events, 0.0 us)
Async XLA Ops:
  0.0 9.5 %copy-start = (bf16[192,128,128]{2,1,0:T(8,128)(2,1)S(1)}, bf16[192,128,128]{2,1,0:T(8,128)(2,1)}, u32[]{:S(2)}) copy-start(bf16[192,128,128]{2,1,0:T(8,128)(2,1)} %param.6) | copy-start | bytes 18874372
  0.0 9.5 %copy-start.2 = (s32[192]{0:T(256)S(1)}, s32[192]{0:T(256)}, u32[]{:S(2)}) copy-start(s32[192]{0:T(256)} %refs_1_.1) | copy-start | bytes 2308
  0.0 9.5 %copy-start.1 = (s32[192]{0:T(256)S(1)}, s32[192]{0:T(256)}, u32[]{:S(2)}) copy-start(s32[192]{0:T(256)} %refs_0_.1) | copy-start | bytes 2308
  0.0 1.5 %collective-permute-start = (bf16[8,512]{1,0:T(8,128)(2,1)}, bf16[8,512]{1,0:T(8,128)(2,1)S(1)}, u32[]{:S(2)}, u32[]{:S(2)}) collective-permute-start(bf16[8,512]{1,0:T(8,128)(2,1)} %param.5), channel_id=1, source_target_pairs={{0,1},{1,0},{2,3},{3,2},{4,5},{5,4},{6,7},{7,6},{8,9},{9,8},{10,11... | collective-permute-start | bytes 24584 | tf_op jit(solution)/shard_map/ppermute | solution.py:124
  1.5 4.9 %collective-permute-start.3 = (bf16[16,512]{1,0:T(8,128)(2,1)S(1)}, bf16[16,512]{1,0:T(8,128)(2,1)S(1)}, u32[]{:S(2)}, u32[]{:S(2)}) collective-permute-start(bf16[16,512]{1,0:T(8,128)(2,1)S(1)} %constant_dynamic-update-slice_fusion.refs_2_), channel_id=1, source_target_pairs={{0,6},{1,7},{2,4},{3,5},{4,2},{5,3},{6,0},{7,1},{8,14},{9,15},{10,... | collective-permute-start | bytes 49160 | tf_op jit(solution)/shard_map/ppermute | solution.py:129
  4.2 5.2 %collective-permute-start.2 = (bf16[16,512]{1,0:T(8,128)(2,1)S(1)}, bf16[16,512]{1,0:T(8,128)(2,1)S(1)}, u32[]{:S(2)}, u32[]{:S(2)}) collective-permute-start(bf16[16,512]{1,0:T(8,128)(2,1)S(1)} %constant_dynamic-update-slice_fusion.refs_2_), channel_id=1, source_target_pairs={{0,4},{1,5},{2,6},{3,7},{4,0},{5,1},{6,2},{7,3},{8,12},{9,13},{10,... | collective-permute-start | bytes 49160 | tf_op jit(solution)/shard_map/ppermute | solution.py:129
  5.0 4.4 %collective-permute-start.1 = (bf16[16,512]{1,0:T(8,128)(2,1)S(1)}, bf16[16,512]{1,0:T(8,128)(2,1)S(1)}, u32[]{:S(2)}, u32[]{:S(2)}) collective-permute-start(bf16[16,512]{1,0:T(8,128)(2,1)S(1)} %constant_dynamic-update-slice_fusion.refs_2_), channel_id=1, source_target_pairs={{0,2},{1,3},{2,0},{3,1},{4,6},{5,7},{6,4},{7,5},{8,10},{9,11},{10,... | collective-permute-start | bytes 49160 | tf_op jit(solution)/shard_map/ppermute | solution.py:129

commit v2 on v1

--- a/solution.py
+++ b/solution.py
@@ -10,7 +10,7 @@
 TILE = 128
 SUB = 8
 GROUP = 48
-PEERS = [4, 12, 24, 2, 28, 10, 18, 27, 21, 9, 19, 8, 6, 17, 13, 15, 29, 3, 5, 1, 7, 14, 0, 31, 20, 30, 26, 22, 25, 11, 23, 16]
+PEERS = [28, 9, 19, 10, 29, 5, 7, 22, 0, 14, 8, 15, 23, 24, 21, 13, 25, 27, 6, 16, 26, 18, 11, 3, 17, 2, 1, 31, 12, 4, 30, 20]
 HOPS = (1, 2, 3)
 F32 = jnp.float32
 

time: 32.9 us -> 31.4 us (0.954)
  blocking collectives: 20.6 us -> 18.9 us
    all_to_all x1, blocking collectives: 20.6 us -> 18.9 us  [per_device(): lax.all_to_all(pieces, 'row', 0, 0, axis_index_groups=[PEERS])]
where the time goes in v2:
time: 31.4 us; the launch traced here: 31 us
  blocking collectives  18.9 us (60%)
  starting transfers between devices  4.19 us (13%)
  waiting for transfers between devices  3.78 us (12%)
  Pallas kernels  2.63 us (8%)
  local copies, waits for them, and re-layouts  0.86 us (3%)
  between operations  0.7 us (2%)
    all_to_all x1, blocking collectives, per_device(): lax.all_to_all(pieces, 'row', 0, 0, axis_index_groups=[PEERS])  18.9 us
    ppermute x3, starting transfers between devices, per_device(): far[hop] = lax.ppermute(pair, 'col', steps)  4.09 us
    ppermute x3, waiting for transfers between devices, per_device(): far[hop] = lax.ppermute(pair, 'col', steps)  3.26 us
    pallas_call x1, Pallas kernels, per_device(): pl.pallas_call(contribution_kernel, out_shape=jax.ShapeDtypeStruct((row_c...  1.92 us
    unnamed x7, local copies, waits for them, and re-layouts  0.86 us
    pallas_call x1, Pallas kernels, per_device(): pl.pallas_call(sum_kernel, out_shape=jax.ShapeDtypeStruct((own_rows, row_...  0.71 us
  transfers between devices with their start and end apart: 4, of which 3 were waited for; matrix products, arithmetic and copies ran while one was open for 3% of the time, Pallas kernels for 0%

profile of v2, /device:TPU:32, one launch (start us, length us, event | category | flops | bytes accessed | tf_op | source)
XLA Modules:
  0.0 31.0 jit_solution(15816802216725600742)
XLA Ops:
  0.0 0.0 copy-start
  0.0 0.0 copy-start.2
  0.0 0.0 copy-start.1
  0.0 0.1 collective-permute-start
  0.1 0.8 %constant_dynamic-update-slice_fusion.1 = bf16[16,512]{1,0:T(8,128)(2,1)S(1)} fusion(bf16[8,512]{1,0:T(8,128)(2,1)} %param.5), kind=kLoop, calls=%fused_computation.1 | loop fusion | bytes 16384
  1.0 0.5 %collective-permute-done = bf16[8,512]{1,0:T(8,128)(2,1)S(1)} collective-permute-done((bf16[8,512]{1,0:T(8,128)(2,1)}, bf16[8,512]{1,0:T(8,128)(2,1)S(1)}, u32[]{:S(2)}, u32[]{:S(2)}) %collective-permute-start) | collective-permute-done | bytes 8224 | tf_op jit(solution)/shard_map/ppermute | solution.py:124
  1.5 2.8 %collective-permute-start.3 = (bf16[16,512]{1,0:T(8,128)(2,1)S(1)}, bf16[16,512]{1,0:T(8,128)(2,1)S(1)}, u32[]{:S(2)}, u32[]{:S(2)}) collective-permute-start(bf16[16,512]{1,0:T(8,128)(2,1)S(1)} %constant_dynamic-update-slice_fusion.refs_2_), channel_id=1, source_target_pairs={{0,6},{1,7},{2,4},{3,5},{4,2},{5,3},{6,0},{7,1},{8,14},{9,15},{10,... | collective-permute-start | bytes 49160 | tf_op jit(solution)/shard_map/ppermute | solution.py:129
  4.2 0.8 %collective-permute-start.2 = (bf16[16,512]{1,0:T(8,128)(2,1)S(1)}, bf16[16,512]{1,0:T(8,128)(2,1)S(1)}, u32[]{:S(2)}, u32[]{:S(2)}) collective-permute-start(bf16[16,512]{1,0:T(8,128)(2,1)S(1)} %constant_dynamic-update-slice_fusion.refs_2_), channel_id=1, source_target_pairs={{0,4},{1,5},{2,6},{3,7},{4,0},{5,1},{6,2},{7,3},{8,12},{9,13},{10,... | collective-permute-start | bytes 49160 | tf_op jit(solution)/shard_map/ppermute | solution.py:129
  5.0 0.5 %collective-permute-start.1 = (bf16[16,512]{1,0:T(8,128)(2,1)S(1)}, bf16[16,512]{1,0:T(8,128)(2,1)S(1)}, u32[]{:S(2)}, u32[]{:S(2)}) collective-permute-start(bf16[16,512]{1,0:T(8,128)(2,1)S(1)} %constant_dynamic-update-slice_fusion.refs_2_), channel_id=1, source_target_pairs={{0,2},{1,3},{2,0},{3,1},{4,6},{5,7},{6,4},{7,5},{8,10},{9,11},{10,... | collective-permute-start | bytes 49160 | tf_op jit(solution)/shard_map/ppermute | solution.py:129
  6.2 0.2 collective-permute-done.3.refs_2_
  6.4 3.1 %collective-permute-done.2.refs_1_ = bf16[16,512]{1,0:T(8,128)(2,1)S(1)} collective-permute-done((bf16[16,512]{1,0:T(8,128)(2,1)S(1)}, bf16[16,512]{1,0:T(8,128)(2,1)S(1)}, u32[]{:S(2)}, u32[]{:S(2)}) %collective-permute-start.2) | collective-permute-done | bytes 16416 | tf_op jit(solution)/shard_map/ppermute | solution.py:129
  9.5 0.0 collective-permute-done.1.refs_0_
  9.5 0.0 copy-done
  9.5 0.0 copy-done.2
  9.5 0.0 copy-done.1
  9.5 1.9 %shard_map.56 = s32[544,128]{1,0:T(8,128)S(1)} custom-call(s32[1]{0:T(128)S(6)} %copy.8.live_ref, s32[192]{0:T(256)S(1)} %copy-done.1, s32[192]{0:T(256)S(1)} %copy-done.2, bf16[16,512]{1,0:T(8,128)(2,1)S(1)} %constant_dynamic-update-slice_fusion.refs_2_, bf16[3,16,512]{2,1,0:T(8,128)(2,1)S(1)} %shard_map.55.refs_3_, bf16[96,256,128]{2,1,0:T(8,128)(2,1)S(1)} %bitcast.4), custom_call_target="tpu_custom_call" | custom-call | tf_op jit(solution)/shard_map/pallas_call | solution.py:139
  11.4 18.9 %all_to_all.5 = s32[32,17,1,128]{3,2,1,0:T(1,128)S(1)} all-to-all(s32[32,17,1,128]{3,2,1,0:T(1,128)S(1)} %bitcast.5), channel_id=1, replica_groups={{224,72,152,80,232,40,56,176,0,112,64,120,184,192,168,104,200,216,48,12..., dimensions={0} | all-to-all | bytes 557056 | tf_op jit(solution)/shard_map/all_to_all | solution.py:154
  30.3 0.7 %shard_map.57 = f32[8,512]{1,0:T(8,128)} custom-call(s32[544,128]{1,0:T(8,128)S(1)} %bitcast.6), custom_call_target="tpu_custom_call" | custom-call | tf_op jit(solution)/shard_map/pallas_call | solution.py:155
  (2 shorter events, 0.0 us)
Async XLA Ops:
  0.0 9.5 %copy-start = (bf16[192,128,128]{2,1,0:T(8,128)(2,1)S(1)}, bf16[192,128,128]{2,1,0:T(8,128)(2,1)}, u32[]{:S(2)}) copy-start(bf16[192,128,128]{2,1,0:T(8,128)(2,1)} %param.6) | copy-start | bytes 18874372
  0.0 9.5 %copy-start.2 = (s32[192]{0:T(256)S(1)}, s32[192]{0:T(256)}, u32[]{:S(2)}) copy-start(s32[192]{0:T(256)} %refs_1_.1) | copy-start | bytes 2308
  0.0 9.5 %copy-start.1 = (s32[192]{0:T(256)S(1)}, s32[192]{0:T(256)}, u32[]{:S(2)}) copy-start(s32[192]{0:T(256)} %refs_0_.1) | copy-start | bytes 2308
  0.0 1.5 %collective-permute-start = (bf16[8,512]{1,0:T(8,128)(2,1)}, bf16[8,512]{1,0:T(8,128)(2,1)S(1)}, u32[]{:S(2)}, u32[]{:S(2)}) collective-permute-start(bf16[8,512]{1,0:T(8,128)(2,1)} %param.5), channel_id=1, source_target_pairs={{0,1},{1,0},{2,3},{3,2},{4,5},{5,4},{6,7},{7,6},{8,9},{9,8},{10,11... | collective-permute-start | bytes 24584 | tf_op jit(solution)/shard_map/ppermute | solution.py:124
  1.5 4.9 %collective-permute-start.3 = (bf16[16,512]{1,0:T(8,128)(2,1)S(1)}, bf16[16,512]{1,0:T(8,128)(2,1)S(1)}, u32[]{:S(2)}, u32[]{:S(2)}) collective-permute-start(bf16[16,512]{1,0:T(8,128)(2,1)S(1)} %constant_dynamic-update-slice_fusion.refs_2_), channel_id=1, source_target_pairs={{0,6},{1,7},{2,4},{3,5},{4,2},{5,3},{6,0},{7,1},{8,14},{9,15},{10,... | collective-permute-start | bytes 49160 | tf_op jit(solution)/shard_map/ppermute | solution.py:129
  4.2 5.2 %collective-permute-start.2 = (bf16[16,512]{1,0:T(8,128)(2,1)S(1)}, bf16[16,512]{1,0:T(8,128)(2,1)S(1)}, u32[]{:S(2)}, u32[]{:S(2)}) collective-permute-start(bf16[16,512]{1,0:T(8,128)(2,1)S(1)} %constant_dynamic-update-slice_fusion.refs_2_), channel_id=1, source_target_pairs={{0,4},{1,5},{2,6},{3,7},{4,0},{5,1},{6,2},{7,3},{8,12},{9,13},{10,... | collective-permute-start | bytes 49160 | tf_op jit(solution)/shard_map/ppermute | solution.py:129
  5.0 4.4 %collective-permute-start.1 = (bf16[16,512]{1,0:T(8,128)(2,1)S(1)}, bf16[16,512]{1,0:T(8,128)(2,1)S(1)}, u32[]{:S(2)}, u32[]{:S(2)}) collective-permute-start(bf16[16,512]{1,0:T(8,128)(2,1)S(1)} %constant_dynamic-update-slice_fusion.refs_2_), channel_id=1, source_target_pairs={{0,2},{1,3},{2,0},{3,1},{4,6},{5,7},{6,4},{7,5},{8,10},{9,11},{10,... | collective-permute-start | bytes 49160 | tf_op jit(solution)/shard_map/ppermute | solution.py:129
